TPU v7x, 32 devices: a whole 2x2x4 slice. The times are simulated.
32 devices in a mesh: lat: 8 (over z, core), lon: 4 (over y, x).
Axes of the slice: x: 2, y: 2, z: 4, core: 2. Of those that a mesh axis runs over, the one named last changes fastest.
Arguments:
- ensemble: float32 [3, 80, 256, 512], P(None, None, 'lat', 'lon'), may hold values from -6 to 6
- courant_cols: float32 [1, 256, 512], P(None, 'lat', 'lon'), may hold values from -0.6 to 0.6
- courant_rows: float32 [1, 256, 512], P(None, 'lat', 'lon'), may hold values from -0.6 to 0.6
- obs_value: float32 [2, 768], P(None, ('lat', 'lon')), may hold values from -8 to 8
- obs_error: float32 [2, 768], P(None, ('lat', 'lon')), may hold values from 0.2 to 2
- obs_cell: int32 [2, 768], P(None, ('lat', 'lon')), may hold values from 0 to 4095
- obs_kind: int32 [2, 768], P(None, ('lat', 'lon')), may hold values from 0 to 2
- obs_live: int32 [2, 768], P(None, ('lat', 'lon')), may hold values from 0 to 1, as said below
- obs_list: int32 [2, 768, 9], P(None, ('lat', 'lon')), may hold values 0 or 1
Outputs:
- analysis: float32 [3, 80, 256, 512], P(None, None, 'lat', 'lon')
Inputs may be any that keep to these rules, and one draw needn't show every extreme that they name: `obs_live`: in each batch the live slots of a tile are its first ones, and in every batch some tile has all 24 slots live.
All inputs are finite; a program needn't handle non-finite values. No bound on the sum of `obs_list` on one device may be relied on, other than what follows from the above.
Results may differ from a plain program's by a relative error of at most 0.0003.
Values sent between devices are 32-bit elements; how exact they have to be, the bound alone decides.
A program may use at most 64 MiB of HBM per device.

v0:
```python
import functools
import jax
import jax.numpy as jnp
from jax import lax
from jax.sharding import PartitionSpec as P
from jax.experimental import pallas as pl
from jax.experimental.pallas import tpu as pltpu

MESH = pl.DeviceIdType.MESH
EXTRA = 16
HIGHEST = lax.Precision.HIGHEST
AROUND = [(a, b) for a in (-1, 0, 1) for b in (-1, 0, 1) if (a, b) != (0, 0)]


def slot_of(a, b):
    return (a + 1) * 3 + b + 1


def taper(dist):
    return jnp.square(jnp.maximum(0.0, 1.0 - jnp.abs(dist)))


def pad_rows(x, rows):
    if rows == x.shape[0]:
        return x
    return jnp.concatenate([x, jnp.zeros((rows - x.shape[0], x.shape[1]), x.dtype)], axis=0)


def table_columns(near, members, trows, tcols):
    rows, cols, factor = [], [], []
    for a in (-1, 0, 1):
        for b in (-1, 0, 1):
            block = near[slot_of(a, b)]
            rows.append(block[:, members + 3 : members + 4] + float(a * trows))
            cols.append(block[:, members + 4 : members + 5] + float(b * tcols))
            took = members + 5 + slot_of(-a, -b)
            factor.append(block[:, members + 1 : members + 2] * block[:, took : took + 1])
    return [jnp.concatenate(part, axis=0) for part in (rows, cols, factor)]


def make_table(prior, info):
    members, lanes = prior.shape
    ybar = jnp.sum(prior, axis=0, keepdims=True) / members
    yp = prior - ybar
    spread = jnp.sum(yp * yp, axis=0, keepdims=True) / (members - 1)
    value, live, error = info[0:1], info[1:2], info[2:3]
    total = spread + error
    gain = live / total
    alpha = 1.0 / (1.0 + jnp.sqrt(error / total))
    innov = value - ybar
    at = lax.broadcasted_iota(jnp.int32, info.shape, 0)
    extra = jnp.where(at == 0, innov, jnp.where(at == 1, gain, jnp.where(at == 2, alpha, info)))
    return jnp.transpose(pad_rows(jnp.concatenate([yp, extra], axis=0), lanes))


def exchange_kernel(
    sizes, x_ref, cu_ref, cv_ref, info_ref, where_ref, state_ref, tables_ref,
    xt, pack, halo, near, row_send, row_recv, col_send, col_recv, tab_send, tab_recv,
):
    fields, members, trows, tcols, slots, n_lat, n_lon = sizes
    lat, lon = lax.axis_index("lat"), lax.axis_index("lon")

    def exists(a, b):
        r, c = lat + a, lon + b
        return (r >= 0) & (r < n_lat) & (c >= 0) & (c < n_lon)

    xt[:, 0] = jnp.zeros((fields, members, tcols), jnp.float32)
    xt[:, trows + 1] = jnp.zeros((fields, members, tcols), jnp.float32)
    halo[...] = jnp.zeros(halo.shape, jnp.float32)
    near[...] = jnp.zeros(near.shape, jnp.float32)

    barrier = pltpu.get_barrier_semaphore()
    for a, b in AROUND:
        @pl.when(exists(a, b))
        def _():
            pl.semaphore_signal(barrier, inc=1, device_id=(lat + a, lon + b), device_id_type=MESH)

    lane = lax.broadcasted_iota(jnp.int32, (members, tcols), 1)

    def turn(i, carry):
        west, east = carry
        for f in range(fields):
            tile = x_ref[pl.ds(f * members * trows + i, members, stride=trows), :]
            xt[f, i + 1] = tile
            at = f * trows + i
            here = lane == at
            west = jnp.where(here, jnp.broadcast_to(tile[:, 0:1], tile.shape), west)
            east = jnp.where(here, jnp.broadcast_to(tile[:, tcols - 1 : tcols], tile.shape), east)
        return west, east

    none = jnp.zeros((members, tcols), jnp.float32)
    west, east = lax.fori_loop(0, trows, turn, (none, none))
    pack[0] = west
    pack[1] = east

    lat_i = jnp.int32(1) * lat
    lat_n = jnp.where(lat_i > 0, 1, 0) + jnp.where(lat_i < n_lat - 1, 1, 0) + 1
    lon_n = jnp.where(lon > 0, 1, 0) + jnp.where(lon < n_lon - 1, 1, 0) + 1
    pl.semaphore_wait(barrier, lat_n * lon_n - 1)

    def row_copy(k):
        return pltpu.make_async_remote_copy(
            src_ref=xt.at[:, 1 if k == 0 else trows],
            dst_ref=xt.at[:, trows + 1 if k == 0 else 0],
            send_sem=row_send.at[k], recv_sem=row_recv.at[k],
            device_id=(lat - 1 if k == 0 else lat + 1, lon), device_id_type=MESH,
        )

    def col_copy(k):
        return pltpu.make_async_remote_copy(
            src_ref=pack.at[k], dst_ref=halo.at[k],
            send_sem=col_send.at[k], recv_sem=col_recv.at[k],
            device_id=(lat, lon - 1 if k == 0 else lon + 1), device_id_type=MESH,
        )

    for k, d in ((0, -1), (1, 1)):
        @pl.when(exists(0, d))
        def _():
            col_copy(k).start()

        @pl.when(exists(d, 0))
        def _():
            row_copy(k).start()

    for k, d in ((0, -1), (1, 1)):
        @pl.when(exists(0, d))
        def _():
            col_copy(k).wait_send()

        @pl.when(exists(d, 0))
        def _():
            row_copy(k).wait_send()

        @pl.when(exists(0, -d))
        def _():
            col_copy(k).wait_recv()

        @pl.when(exists(-d, 0))
        def _():
            row_copy(k).wait_recv()

    def advect(i, carry):
        u = jnp.broadcast_to(cu_ref[pl.ds(i, 1), :], (members, tcols))
        v = jnp.broadcast_to(cv_ref[pl.ds(i, 1), :], (members, tcols))
        hu, hv = 0.5 * u, 0.5 * v
        huu, hvv = hu * u, hv * v
        for f in range(fields):
            mid = xt[f, i + 1]
            south = xt[f, i]
            north = xt[f, i + 2]
            at = f * trows + i
            after = pltpu.roll(halo[0], tcols - 1 - at, 1)
            before = pltpu.roll(halo[1], lax.rem(tcols - at, tcols), 1)
            east = jnp.where(lane == tcols - 1, after, pltpu.roll(mid, tcols - 1, 1))
            west = jnp.where(lane == 0, before, pltpu.roll(mid, 1, 1))
            two = 2.0 * mid
            out = mid - hu * (east - west) + huu * (east - two + west)
            out = out - hv * (north - south) + hvv * (north - two + south)
            state_ref[f * trows + i] = out
        return carry

    lax.fori_loop(0, trows, advect, 0)

    def gather(batch):
        def one(s, prior):
            tile = state_ref[where_ref[batch, 0, s]]
            picked = jnp.where(lane == where_ref[batch, 1, s], tile, 0.0)
            column = jnp.sum(picked, axis=1, keepdims=True)
            return jnp.where(lane == s, jnp.broadcast_to(column, tile.shape), prior)

        return lax.fori_loop(0, slots, one, none)

    def table_copy(batch, a, b):
        return pltpu.make_async_remote_copy(
            src_ref=near.at[batch, slot_of(0, 0)],
            dst_ref=near.at[batch, slot_of(-a, -b)],
            send_sem=tab_send.at[batch, slot_of(a, b)],
            recv_sem=tab_recv.at[batch, slot_of(-a, -b)],
            device_id=(lat + a, lon + b), device_id_type=MESH,
        )

    def send(batch):
        for a, b in AROUND:
            @pl.when(exists(a, b))
            def _():
                table_copy(batch, a, b).start()

    def finish(batch):
        for a, b in AROUND:
            @pl.when(exists(a, b))
            def _():
                table_copy(batch, a, b).wait_send()

            @pl.when(exists(-a, -b))
            def _():
                table_copy(batch, a, b).wait_recv()

    near[0, slot_of(0, 0)] = make_table(gather(0), info_ref[0])[:slots]
    send(0)
    later = gather(1)
    finish(0)

    info = info_ref[1]
    board = [near[0, k] for k in range(9)]
    rows, cols, factor = table_columns(board, members, trows, tcols)
    whole = jnp.concatenate(board, axis=0)
    count = whole.shape[0]
    loc = taper((rows - info[3:4]) / trows) * factor * taper((cols - info[4:5]) / trows)
    mean = jnp.sum(later, axis=0, keepdims=True) / members
    pert = later - mean
    shut = lax.broadcasted_iota(jnp.int32, whole.shape, 1)
    yp = jnp.where(shut < members, whole, 0.0)
    proj = jnp.dot(yp, pad_rows(pert, tcols), precision=HIGHEST, preferred_element_type=jnp.float32)
    weight = proj * loc * (1.0 / (members - 1))
    mean = mean + jnp.sum(weight * whole[:, members : members + 1], axis=0, keepdims=True)
    scaled = whole * whole[:, members + 2 : members + 3]
    full = -(-count // tcols) * tcols
    change = jnp.dot(
        jnp.transpose(pad_rows(scaled, full))[:members], pad_rows(weight, full),
        precision=HIGHEST, preferred_element_type=jnp.float32,
    )
    near[1, slot_of(0, 0)] = make_table(mean + pert - change, info)[:slots]
    send(1)
    finish(1)
    tables_ref[...] = near[...]


def split(x):
    hi = x.astype(jnp.bfloat16)
    return hi, (x - hi.astype(jnp.float32)).astype(jnp.bfloat16)


def update_kernel(sizes, state_ref, tables_ref, out_ref, left, back, rowrel, colw):
    fields, members, trows, tcols, slots, high = sizes
    count = 9 * slots
    depth = left.shape[1]
    wide = left.shape[2]
    tall = back.shape[1] // 2
    step = pl.program_id(0)

    @pl.when(step == 0)
    def _():
        for batch in range(2):
            board = [tables_ref[batch, k] for k in range(9)]
            rows, cols, factor = table_columns(board, members, trows, tcols)
            whole = jnp.concatenate(board, axis=0)
            lane = lax.broadcasted_iota(jnp.int32, whole.shape, 1)
            yp = jnp.where(lane < members, whole, 0.0)
            hi = yp.astype(jnp.bfloat16).astype(jnp.float32)
            lo = yp - hi
            lo_at = pltpu.roll(lo, members, 1)
            first = jnp.where(lane < members, hi, lo_at)
            second = jnp.where(lane < 2 * members - tcols, lo_at, pltpu.roll(hi, 2 * members - tcols, 1))
            both = jnp.concatenate([first, second], axis=1)
            left[batch] = pad_rows(both, depth).astype(jnp.bfloat16)
            full = -(-depth // tcols) * tcols
            turned = jnp.transpose(pad_rows(whole, full))[:tall]
            alpha = jnp.transpose(pad_rows(whole, full))[members + 2 : members + 3]
            at = lax.broadcasted_iota(jnp.int32, turned.shape, 0)
            scaled = jnp.where(at < members, -alpha * turned, jnp.where(at == members, turned, 0.0))
            hi, lo = split(scaled)
            back[batch, 0:tall] = hi[:, :depth]
            back[batch, tall:] = lo[:, :depth]
            column = lax.broadcasted_iota(jnp.int32, whole.shape, 1).astype(jnp.float32)
            near_w = taper((cols - column) / trows) * (factor * (1.0 / (members - 1)))
            colw[batch] = pad_rows(near_w, depth)
            rowrel[batch] = pad_rows(jnp.broadcast_to(rows, whole.shape), depth)

    lines = out_ref.reshape(fields * members * high, tcols)
    zeros = jnp.zeros((wide - 3 * members, 2 * tcols), jnp.bfloat16)

    def pair(p, carry):
        row = step * high + 2 * p
        loc = []
        for batch in range(2):
            parts = []
            for d in range(2):
                z = (rowrel[batch] - (row + d).astype(jnp.float32)) * (1.0 / trows)
                parts.append(taper(z) * colw[batch])
            loc.append(jnp.concatenate(parts, axis=1))
        for f in range(fields):
            x = jnp.concatenate([state_ref[f, 2 * p], state_ref[f, 2 * p + 1]], axis=1)
            mean = jnp.sum(x, axis=0, keepdims=True) * (1.0 / members)
            pert = x - mean
            for batch in range(2):
                hi, lo = split(pert)
                right = jnp.concatenate([hi, hi, lo, zeros], axis=0)
                proj = jnp.dot(left[batch], right, preferred_element_type=jnp.float32)
                w_hi, w_lo = split(proj * loc[batch])
                one = jnp.dot(back[batch], w_hi, preferred_element_type=jnp.float32)
                two = jnp.dot(back[batch, 0:tall], w_lo, preferred_element_type=jnp.float32)
                change = one[:tall] + one[tall:] + two
                pert = pert + change[:members]
                mean = mean + change[members : members + 1]
            x = mean + pert
            for d in range(2):
                lines[pl.ds(f * members * high + 2 * p + d, members, stride=high), :] = x[:, d * tcols : (d + 1) * tcols]
        return carry

    lax.fori_loop(0, high // 2, pair, 0)


def on_device(n_lat, n_lon, ensemble, courant_cols, courant_rows, obs_value, obs_error, obs_cell, obs_kind, obs_live, obs_list):
    fields, members, trows, tcols = ensemble.shape
    slots = obs_value.shape[1]
    f32 = jnp.float32
    row, col = obs_cell // tcols, obs_cell % tcols
    info = jnp.concatenate(
        [jnp.stack([obs_value, obs_live.astype(f32), obs_error, row.astype(f32), col.astype(f32)], axis=1),
         jnp.swapaxes(obs_list, 1, 2).astype(f32)], axis=1)
    info = jnp.pad(info, ((0, 0), (0, EXTRA - info.shape[1]), (0, tcols - slots)), constant_values=1.0)
    place = jnp.stack([obs_kind * trows + row, col], axis=1)
    vmem = pl.BlockSpec(memory_space=pltpu.VMEM)
    state, tables = pl.pallas_call(
        functools.partial(exchange_kernel, (fields, members, trows, tcols, slots, n_lat, n_lon)),
        out_shape=(
            jax.ShapeDtypeStruct((fields * trows, members, tcols), f32),
            jax.ShapeDtypeStruct((2, 9, slots, tcols), f32),
        ),
        in_specs=[vmem] * 4 + [pl.BlockSpec(memory_space=pltpu.SMEM)],
        out_specs=(vmem, vmem),
        scratch_shapes=[
            pltpu.VMEM((fields, trows + 2, members, tcols), f32),
            pltpu.VMEM((2, members, tcols), f32),
            pltpu.VMEM((2, members, tcols), f32),
            pltpu.VMEM((2, 9, slots, tcols), f32),
        ] + [pltpu.SemaphoreType.DMA((2,))] * 4 + [pltpu.SemaphoreType.DMA((2, 9))] * 2,
        compiler_params=pltpu.CompilerParams(
            collective_id=0, has_side_effects=True, vmem_limit_bytes=40 * 2**20),
        name="exchange",
    )(ensemble.reshape(fields * members * trows, tcols), courant_cols[0], courant_rows[0], info, place)

    high = 8
    depth = -(-9 * slots // 16) * 16
    tall = -(-(members + 1) // 16) * 16
    wide = -(-3 * members // tcols) * tcols
    return pl.pallas_call(
        functools.partial(update_kernel, (fields, members, trows, tcols, slots, high)),
        grid=(trows // high,),
        out_shape=jax.ShapeDtypeStruct(ensemble.shape, f32),
        in_specs=[
            pl.BlockSpec((fields, high, members, tcols), lambda i: (0, i, 0, 0)),
            pl.BlockSpec((2, 9, slots, tcols), lambda i: (0, 0, 0, 0)),
        ],
        out_specs=pl.BlockSpec((fields, members, high, tcols), lambda i: (0, 0, i, 0)),
        scratch_shapes=[
            pltpu.VMEM((2, depth, wide), jnp.bfloat16),
            pltpu.VMEM((2, 2 * tall, depth), jnp.bfloat16),
            pltpu.VMEM((2, depth, tcols), f32),
            pltpu.VMEM((2, depth, tcols), f32),
        ],
        compiler_params=pltpu.CompilerParams(vmem_limit_bytes=40 * 2**20),
        name="update",
    )(state.reshape(fields, trows, members, tcols), tables)


def solution(mesh):
    placed = (
        P(None, None, "lat", "lon"),
        P(None, "lat", "lon"),
        P(None, "lat", "lon"),
        P(None, ("lat", "lon")),
        P(None, ("lat", "lon")),
        P(None, ("lat", "lon")),
        P(None, ("lat", "lon")),
        P(None, ("lat", "lon")),
        P(None, ("lat", "lon"), None),
    )
    return jax.shard_map(
        functools.partial(on_device, mesh.shape["lat"], mesh.shape["lon"]),
        mesh=mesh,
        in_specs=placed,
        out_specs=P(None, None, "lat", "lon"),
        check_vma=False,
    )
```

profile of v0, /device:TPU:1, one launch (start us, length us, event | category | flops | bytes accessed | tf_op | source)
XLA Modules:
  0.0 68.7 jit_solution(11183758914776099561)
XLA Ops:
  0.0 0.7 convert_element_type.15
  0.7 0.7 %fusion.1 = (f32[2,24]{1,0:T(2,128)S(1)}, s32[2,24]{1,0:T(2,128)S(1)}, s32[2,24]{1,0:T(2,128)S(1)}, s32[2,24]{1,0:T(2,128)S(1)}) fusion(s32[2,24]{1,0:T(2,128)} %param.14, s32[2,24]{1,0:T(2,128)} %param.15), kind=kLoop, calls=%fused_computation.11 | loop fusion | flops 1056 | bytes 1152 | tf_op jit(solution)/shard_map/convert_element_type | solution.py:309
  1.4 0.7 %fusion = f32[2,9,24]{2,1,0:T(8,128)S(1)} fusion(s32[2,24,9]{1,0,2:T(2,128)} %param.17), kind=kLoop, calls=%fused_computation.1 | loop fusion | flops 432 | bytes 3456 | tf_op jit(solution)/shard_map/convert_element_type | solution.py:310
  2.1 0.8 %concatenate.3 = f32[2,14,24]{2,1,0:T(8,128)S(1)} concatenate(f32[2,1,24]{2,1,0:T(1,128)} %bitcast.36, f32[2,1,24]{2,1,0:T(1,128)S(1)} %bitcast.31, f32[2,1,24]{2,1,0:T(1,128)} %bitcast.37, f32[2,1,24]{2,1,0:T(1,128)S(1)} %bitcast.32, f32[2,1,24]{2,1,0:T(1,128)S(1)} %bitcast.33, f32[2,9,24]{2,1,0:T(8,128)S(1)} %fusion), dimensions={1} | concatenate | bytes 5376 | tf_op jit(solution)/shard_map/concatenate | solution.py:308
  3.0 0.0 copy-start
  3.0 2.1 %copy-done = f32[3,80,32,128]{3,2,1,0:T(8,128)S(1)} copy-done((f32[3,80,32,128]{3,2,1,0:T(8,128)S(1)}, f32[3,80,32,128]{3,2,1,0:T(8,128)}, u32[]{:S(2)}) %copy-start) | copy-done | bytes 3932184
  5.1 0.0 copy-start.1
  5.1 0.7 %copy-done.1 = f32[1,32,128]{2,1,0:T(8,128)S(1)} copy-done((f32[1,32,128]{2,1,0:T(8,128)S(1)}, f32[1,32,128]{2,1,0:T(8,128)}, u32[]{:S(2)}) %copy-start.1) | copy-done | bytes 16408
  5.8 0.0 copy-start.2
  5.8 0.7 %copy-done.2 = f32[1,32,128]{2,1,0:T(8,128)S(1)} copy-done((f32[1,32,128]{2,1,0:T(8,128)S(1)}, f32[1,32,128]{2,1,0:T(8,128)}, u32[]{:S(2)}) %copy-start.2) | copy-done | bytes 16408
  6.5 29.7 %exchange.1 = (f32[96,80,128]{2,1,0:T(8,128)S(1)}, f32[2,9,24,128]{3,2,1,0:T(8,128)S(1)}) custom-call(f32[7680,128]{1,0:T(8,128)S(1)} %bitcast.28, f32[32,128]{1,0:T(8,128)S(1)} %bitcast.29, f32[32,128]{1,0:T(8,128)S(1)} %bitcast.30, f32[2,16,128]{2,1,0:T(8,128)S(1)} %pad.4.info_ref, s32[2,2,24]{2,1,0:T(2,128)S(1)} %pad_add_fusion.where_ref), custom_call_target="tpu_custom_call" | custom-call | tf_op jit(solution)/shard_map/exchange/pallas_call | solution.py:314
  36.2 32.5 %update.1 = f32[3,80,32,128]{3,2,1,0:T(8,128)} custom-call(f32[3,32,80,128]{3,2,1,0:T(8,128)S(1)} %bitcast.27, f32[2,9,24,128]{3,2,1,0:T(8,128)S(1)} %get-tuple-element.8.tables_ref), custom_call_target="tpu_custom_call" | custom-call | tf_op jit(solution)/shard_map/update/pallas_call | solution.py:337
  (3 shorter events, 0.0 us)
Async XLA Ops:
  3.0 2.1 %copy-start = (f32[3,80,32,128]{3,2,1,0:T(8,128)S(1)}, f32[3,80,32,128]{3,2,1,0:T(8,128)}, u32[]{:S(2)}) copy-start(f32[3,80,32,128]{3,2,1,0:T(8,128)} %param.9) | copy-start | bytes 11796484
  5.1 0.7 %copy-start.1 = (f32[1,32,128]{2,1,0:T(8,128)S(1)}, f32[1,32,128]{2,1,0:T(8,128)}, u32[]{:S(2)}) copy-start(f32[1,32,128]{2,1,0:T(8,128)} %param.10) | copy-start | bytes 49156
  5.8 0.7 %copy-start.2 = (f32[1,32,128]{2,1,0:T(8,128)S(1)}, f32[1,32,128]{2,1,0:T(8,128)}, u32[]{:S(2)}) copy-start(f32[1,32,128]{2,1,0:T(8,128)} %param.11) | copy-start | bytes 49156
where the time goes:
time: 69.2 us; the launch traced here: 68.7 us
  Pallas kernels  62.2 us (90%)
  local copies, waits for them, and re-layouts  4.38 us (6%)
  other arithmetic  2.1 us (3%)
    pallas_call x1, Pallas kernels, on_device(): pl.pallas_call(functools.partial(update_kernel, (fields, members, trows,...  32.5 us
    pallas_call x1, Pallas kernels, on_device(): pl.pallas_call(functools.partial(exchange_kernel, (fields, members, trows...  29.7 us
    unnamed x6, local copies, waits for them, and re-layouts  3.54 us

commit v1 on v0

v1 whole, which is shorter than its diff:
```python
import functools
import jax
import jax.numpy as jnp
from jax import lax
from jax.sharding import PartitionSpec as P
from jax.experimental import pallas as pl
from jax.experimental.pallas import tpu as pltpu

MESH = pl.DeviceIdType.MESH
EXTRA = 16
HIGHEST = lax.Precision.HIGHEST
AROUND = [(a, b) for a in (-1, 0, 1) for b in (-1, 0, 1) if (a, b) != (0, 0)]


def slot_of(a, b):
    return (a + 1) * 3 + b + 1


def taper(dist):
    return jnp.square(jnp.maximum(0.0, 1.0 - jnp.abs(dist)))


def pad_rows(x, rows):
    if rows == x.shape[0]:
        return x
    return jnp.concatenate([x, jnp.zeros((rows - x.shape[0], x.shape[1]), x.dtype)], axis=0)


def table_columns(near, members, trows, tcols):
    rows, cols, factor = [], [], []
    for a in (-1, 0, 1):
        for b in (-1, 0, 1):
            block = near[slot_of(a, b)]
            rows.append(block[:, members + 3 : members + 4] + float(a * trows))
            cols.append(block[:, members + 4 : members + 5] + float(b * tcols))
            took = members + 5 + slot_of(-a, -b)
            factor.append(block[:, members + 1 : members + 2] * block[:, took : took + 1])
    return [jnp.concatenate(part, axis=0) for part in (rows, cols, factor)]


def make_table(prior, info):
    members, lanes = prior.shape
    ybar = jnp.sum(prior, axis=0, keepdims=True) / members
    yp = prior - ybar
    spread = jnp.sum(yp * yp, axis=0, keepdims=True) / (members - 1)
    value, live, error = info[0:1], info[1:2], info[2:3]
    total = spread + error
    gain = live / total
    alpha = 1.0 / (1.0 + jnp.sqrt(error / total))
    innov = value - ybar
    at = lax.broadcasted_iota(jnp.int32, info.shape, 0)
    extra = jnp.where(at == 0, innov, jnp.where(at == 1, gain, jnp.where(at == 2, alpha, info)))
    return jnp.transpose(pad_rows(jnp.concatenate([yp, extra], axis=0), lanes))


def exchange_kernel(
    sizes, x_hbm, cu_hbm, cv_hbm, value_hbm, error_hbm, live_hbm, cell_hbm, list_hbm, cell_ref, kind_ref,
    state_ref, sides_ref, tables_ref,
    x_ref, cu_ref, cv_ref, value_ref, error_ref, live_ref, cells_ref, list_ref, info, listed,
    xt, pack, halo, near, in_sem, row_send, row_recv, col_send, col_recv, tab_send, tab_recv,
):
    fields, members, trows, tcols, slots, n_lat, n_lon = sizes
    lat, lon = lax.axis_index("lat"), lax.axis_index("lon")

    def exists(a, b):
        r, c = lat + a, lon + b
        return (r >= 0) & (r < n_lat) & (c >= 0) & (c < n_lon)

    loads = [
        pltpu.make_async_copy(src, dst, in_sem.at[k])
        for k, (src, dst) in enumerate([
            (x_hbm, x_ref), (cu_hbm, cu_ref), (cv_hbm, cv_ref), (value_hbm, value_ref), (error_hbm, error_ref),
            (live_hbm, live_ref), (cell_hbm, cells_ref), (list_hbm, list_ref)])
    ]
    for copy in loads:
        copy.start()

    xt[:, 0] = jnp.zeros((fields, members, tcols), jnp.float32)
    xt[:, trows + 1] = jnp.zeros((fields, members, tcols), jnp.float32)
    halo[...] = jnp.zeros(halo.shape, jnp.float32)
    near[...] = jnp.zeros(near.shape, jnp.float32)
    info[...] = jnp.ones(info.shape, jnp.float32)
    listed[...] = jnp.zeros(listed.shape, jnp.float32)

    barrier = pltpu.get_barrier_semaphore()
    for a, b in AROUND:
        @pl.when(exists(a, b))
        def _():
            pl.semaphore_signal(barrier, inc=1, device_id=(lat + a, lon + b), device_id_type=MESH)

    lane = lax.broadcasted_iota(jnp.int32, (members, tcols), 1)
    for copy in loads:
        copy.wait()

    def turn(i, carry):
        west, east = carry
        for f in range(fields):
            tile = x_ref[pl.ds(f * members * trows + i, members, stride=trows), :]
            xt[f, i + 1] = tile
            here = lane == f * trows + i
            west = jnp.where(here, jnp.broadcast_to(tile[:, 0:1], tile.shape), west)
            east = jnp.where(here, jnp.broadcast_to(tile[:, tcols - 1 : tcols], tile.shape), east)
        return west, east

    none = jnp.zeros((members, tcols), jnp.float32)
    west, east = lax.fori_loop(0, trows, turn, (none, none), unroll=2)
    pack[0] = west
    pack[1] = east

    lat_n = jnp.where(lat > 0, 1, 0) + jnp.where(lat < n_lat - 1, 1, 0) + 1
    lon_n = jnp.where(lon > 0, 1, 0) + jnp.where(lon < n_lon - 1, 1, 0) + 1
    pl.semaphore_wait(barrier, lat_n * lon_n - 1)

    def row_copy(k):
        return pltpu.make_async_remote_copy(
            src_ref=xt.at[:, 1 if k == 0 else trows],
            dst_ref=xt.at[:, trows + 1 if k == 0 else 0],
            send_sem=row_send.at[k], recv_sem=row_recv.at[k],
            device_id=(lat - 1 if k == 0 else lat + 1, lon), device_id_type=MESH,
        )

    def col_copy(k):
        return pltpu.make_async_remote_copy(
            src_ref=pack.at[k], dst_ref=halo.at[k],
            send_sem=col_send.at[k], recv_sem=col_recv.at[k],
            device_id=(lat, lon - 1 if k == 0 else lon + 1), device_id_type=MESH,
        )

    for k, d in ((0, -1), (1, 1)):
        @pl.when(exists(0, d))
        def _():
            col_copy(k).start()

        @pl.when(exists(d, 0))
        def _():
            row_copy(k).start()

    def advect(i, carry):
        u = jnp.broadcast_to(cu_ref[0, pl.ds(i, 1), :], (members, tcols))
        v = jnp.broadcast_to(cv_ref[0, pl.ds(i, 1), :], (members, tcols))
        hu, hv = 0.5 * u, 0.5 * v
        huu, hvv = hu * u, hv * v
        for f in range(fields):
            mid = xt[f, i + 1]
            south = xt[f, i]
            north = xt[f, i + 2]
            east = jnp.where(lane == tcols - 1, 0.0, pltpu.roll(mid, tcols - 1, 1))
            west = jnp.where(lane == 0, 0.0, pltpu.roll(mid, 1, 1))
            two = 2.0 * mid
            out = mid - hu * (east - west) + huu * (east - two + west)
            out = out - hv * (north - south) + hvv * (north - two + south)
            state_ref[f * trows + i] = out
        return carry

    lax.fori_loop(1, trows - 1, advect, 0)

    for batch in range(2):
        own = pl.ds(0, slots)
        cells = cells_ref[batch : batch + 1, :]
        info[batch, 0:1, own] = value_ref[batch : batch + 1, :]
        info[batch, 1:2, own] = live_ref[batch : batch + 1, :].astype(jnp.float32)
        info[batch, 2:3, own] = error_ref[batch : batch + 1, :]
        row = jnp.floor((cells.astype(jnp.float32) + 0.5) * (1.0 / tcols))
        info[batch, 3:4, own] = row
        info[batch, 4:5, own] = cells.astype(jnp.float32) - row * tcols
        listed[batch, :, 0 : list_ref.shape[2]] = list_ref[batch].astype(jnp.float32)

    def along(column):
        spread = jnp.broadcast_to(column, (trows, tcols))
        line = jnp.transpose(pad_rows(spread, tcols))[0:1]
        total = line
        for f in range(1, fields):
            total = total + pltpu.roll(jnp.broadcast_to(line, (8, tcols)), f * trows, 1)[0:1]
        return total

    u = cu_ref[0]
    rise = along((0.5 * u + 0.5 * u * u)[:, 0:1])
    fall = along((0.5 * u * u - 0.5 * u)[:, tcols - 1 : tcols])

    for k, d in ((0, -1), (1, 1)):
        @pl.when(exists(0, d))
        def _():
            col_copy(k).wait_send()

        @pl.when(exists(d, 0))
        def _():
            row_copy(k).wait_send()

        @pl.when(exists(0, -d))
        def _():
            col_copy(k).wait_recv()

        @pl.when(exists(-d, 0))
        def _():
            row_copy(k).wait_recv()

    advect(0, 0)
    advect(trows - 1, 0)
    first_add = halo[1] * rise
    last_add = halo[0] * fall
    sides_ref[0] = first_add
    sides_ref[1] = last_add

    def gather(batch):
        prior = none
        for s in range(slots):
            cell = cell_ref[batch, s]
            col = lax.rem(cell, tcols)
            at = kind_ref[batch, s] * trows + lax.div(cell, tcols)
            tile = state_ref[at]
            here = lane == at
            picked = jnp.where(lane == col, tile, 0.0)
            picked = picked + jnp.where(here & (col == 0), first_add, 0.0)
            picked = picked + jnp.where(here & (col == tcols - 1), last_add, 0.0)
            column = jnp.sum(picked, axis=1, keepdims=True)
            prior = jnp.where(lane == s, jnp.broadcast_to(column, tile.shape), prior)
        return prior

    def table_copy(batch, a, b):
        return pltpu.make_async_remote_copy(
            src_ref=near.at[batch, slot_of(0, 0)],
            dst_ref=near.at[batch, slot_of(-a, -b)],
            send_sem=tab_send.at[batch, slot_of(a, b)],
            recv_sem=tab_recv.at[batch, slot_of(-a, -b)],
            device_id=(lat + a, lon + b), device_id_type=MESH,
        )

    def send(batch, prior):
        table = make_table(prior, info[batch])[:slots]
        at = lax.broadcasted_iota(jnp.int32, table.shape, 1)
        table = jnp.where(at < members + 5, table, pltpu.roll(listed[batch], members + 5, 1))
        near[batch, slot_of(0, 0)] = table
        for a, b in AROUND:
            @pl.when(exists(a, b))
            def _():
                table_copy(batch, a, b).start()

    def finish(batch):
        for a, b in AROUND:
            @pl.when(exists(a, b))
            def _():
                table_copy(batch, a, b).wait_send()

            @pl.when(exists(-a, -b))
            def _():
                table_copy(batch, a, b).wait_recv()

    send(0, gather(0))
    later = gather(1)
    finish(0)

    board = [near[0, k] for k in range(9)]
    rows, cols, factor = table_columns(board, members, trows, tcols)
    whole = jnp.concatenate(board, axis=0)
    count = whole.shape[0]
    loc = taper((rows - info[1, 3:4]) / trows) * factor * taper((cols - info[1, 4:5]) / trows)
    mean = jnp.sum(later, axis=0, keepdims=True) / members
    pert = later - mean
    shut = lax.broadcasted_iota(jnp.int32, whole.shape, 1)
    yp = jnp.where(shut < members, whole, 0.0)
    proj = jnp.dot(yp, pad_rows(pert, tcols), precision=HIGHEST, preferred_element_type=jnp.float32)
    weight = proj * loc * (1.0 / (members - 1))
    mean = mean + jnp.sum(weight * whole[:, members : members + 1], axis=0, keepdims=True)
    scaled = whole * whole[:, members + 2 : members + 3]
    full = -(-count // tcols) * tcols
    change = jnp.dot(
        jnp.transpose(pad_rows(scaled, full))[:members], pad_rows(weight, full),
        precision=HIGHEST, preferred_element_type=jnp.float32,
    )
    send(1, mean + pert - change)
    finish(1)
    tables_ref[...] = near[...]


def split(x):
    hi = x.astype(jnp.bfloat16)
    return hi, (x - hi.astype(jnp.float32)).astype(jnp.bfloat16)


def beside(parts, rows, lanes):
    width = parts[0][1]
    total = [jnp.zeros((rows, lanes), jnp.float32) for _ in range(2)]
    at = lax.broadcasted_iota(jnp.int32, (rows, lanes), 1)
    for k, (part, _) in enumerate(parts):
        start = k * width
        turned = pltpu.roll(part, start % lanes, 1) if start % lanes else part
        for block in range(2):
            lower, upper = start - block * lanes, start + width - block * lanes
            if upper > 0 and lower < lanes:
                total[block] = jnp.where((at >= lower) & (at < upper), turned, total[block])
    return jnp.concatenate(total, axis=1)


def update_kernel(sizes, state_ref, sides_ref, tables_ref, out_ref, left, back, back3, back2, rowrel, colw, active_ref):
    fields, members, trows, tcols, slots, high = sizes
    depth = left.shape[1]
    wide = left.shape[2]
    tall = back.shape[1] // 2
    third = 2 * tcols // 48 * 16
    step = pl.program_id(0)

    @pl.when(step == 0)
    def _():
        for batch in range(2):
            board = [tables_ref[batch, k] for k in range(9)]
            rows, cols, factor = table_columns(board, members, trows, tcols)
            whole = jnp.concatenate(board, axis=0)
            lane = lax.broadcasted_iota(jnp.int32, whole.shape, 1)
            reach = (
                (factor != 0.0) & (rows > -trows) & (rows < 2 * trows - 1)
                & (cols > -trows) & (cols < tcols - 1 + trows)
            )
            active = jnp.where(reach, 1.0, 0.0)
            whole = jnp.where(lane == members + 1, factor * (1.0 / (members - 1)), whole)
            whole = jnp.where(lane == members + 3, rows, whole)
            whole = jnp.where(lane == members + 4, cols, whole)
            whole = jnp.where(lane == members + 5, active, whole)
            full = -(-depth // tcols) * tcols
            whole = pad_rows(whole, full)
            flags = jnp.transpose(whole)[members + 5 : members + 6]
            r = lax.broadcasted_iota(jnp.int32, (full, full), 0)
            c = lax.broadcasted_iota(jnp.int32, (full, full), 1)
            upper = jnp.where(r <= c, 1.0, 0.0).astype(jnp.bfloat16)
            line = jnp.broadcast_to(flags, (16, full)).astype(jnp.bfloat16)
            running = jnp.dot(line, upper, preferred_element_type=jnp.float32)[0:1]
            active_ref[batch] = jnp.max(running).astype(jnp.int32)
            pick = jnp.where((running - 1.0 == r.astype(jnp.float32)) & (flags > 0.5), 1.0, 0.0)
            whole = jnp.dot(pick, whole, precision=HIGHEST, preferred_element_type=jnp.float32)

            lane = lax.broadcasted_iota(jnp.int32, whole.shape, 1)
            yp = jnp.where(lane < members, whole, 0.0)
            hi = yp.astype(jnp.bfloat16).astype(jnp.float32)
            lo = yp - hi
            both = beside([(hi, members), (lo, members), (hi, members)], full, tcols)
            left[batch] = both[:depth].astype(jnp.bfloat16)
            turned = jnp.transpose(whole)
            alpha = turned[members + 2 : members + 3]
            turned = turned[:tall]
            at = lax.broadcasted_iota(jnp.int32, turned.shape, 0)
            scaled = jnp.where(at < members, -alpha * turned, jnp.where(at == members, turned, 0.0))
            hi, lo = split(scaled)
            back[batch, 0:tall] = hi[:, :depth]
            back[batch, tall:] = lo[:, :depth]
            hi = hi.astype(jnp.float32)[:, :tcols]
            lo = lo.astype(jnp.float32)[:, :tcols]
            back3[batch] = beside([(hi, third), (lo, third), (hi, third)], tall, tcols).astype(jnp.bfloat16)
            back2[batch, 0:tall] = jnp.concatenate([hi, hi], axis=1).astype(jnp.bfloat16)
            back2[batch, tall:] = jnp.concatenate([lo, jnp.zeros_like(lo)], axis=1).astype(jnp.bfloat16)
            column = lane.astype(jnp.float32)
            near_w = taper((whole[:, members + 4 : members + 5] - column) / trows) * whole[:, members + 1 : members + 2]
            colw[batch] = near_w[:depth]
            rowrel[batch] = jnp.broadcast_to(whole[:, members + 3 : members + 4], whole.shape)[:depth]

    lines = out_ref.reshape(fields * members * high, tcols)
    lane = lax.broadcasted_iota(jnp.int32, (members, tcols), 1)

    def run(taken):
        def zero_rows(rows):
            return [jnp.zeros((rows, 2 * tcols), jnp.bfloat16)] if rows else []

        def pair(p, carry):
            row = step * high + 2 * p
            loc = []
            for batch in range(2):
                parts = []
                for d in range(2):
                    z = (rowrel[batch, 0:taken] - (row + d).astype(jnp.float32)) * (1.0 / trows)
                    parts.append(taper(z) * colw[batch, 0:taken])
                loc.append(jnp.concatenate(parts, axis=1))
            xs = []
            for f in range(fields):
                tiles = []
                for d in range(2):
                    at = f * trows + row + d
                    first = pltpu.roll(sides_ref[0], lax.rem(tcols - at, tcols), 1)
                    last = pltpu.roll(sides_ref[1], tcols - 1 - at, 1)
                    add = jnp.where(lane == 0, first, jnp.where(lane == tcols - 1, last, 0.0))
                    tiles.append(state_ref[f, 2 * p + d] + add)
                xs.append(jnp.concatenate(tiles, axis=1))
            means = [jnp.sum(x, axis=0, keepdims=True) * (1.0 / members) for x in xs]
            perts = [x - mean for x, mean in zip(xs, means)]
            for batch in range(2):
                projs = []
                for f in range(fields):
                    hi, lo = split(perts[f])
                    right = jnp.concatenate([hi, hi, lo] + zero_rows(wide - 3 * members), axis=0)
                    projs.append(jnp.dot(left[batch, 0:taken], right, preferred_element_type=jnp.float32))
                for f in range(fields):
                    w_hi, w_lo = split(projs[f] * loc[batch])
                    if taken == third:
                        stack = jnp.concatenate([w_hi, w_hi, w_lo] + zero_rows(2 * tcols - 3 * third), axis=0)
                        change = jnp.dot(back3[batch], stack, preferred_element_type=jnp.float32)
                    elif taken == tcols:
                        stack = jnp.concatenate([w_hi, w_lo], axis=0)
                        one = jnp.dot(back2[batch], stack, preferred_element_type=jnp.float32)
                        change = one[:tall] + one[tall:]
                    else:
                        one = jnp.dot(back[batch], w_hi, preferred_element_type=jnp.float32)
                        two = jnp.dot(back[batch, 0:tall], w_lo, preferred_element_type=jnp.float32)
                        change = one[:tall] + one[tall:] + two
                    perts[f] = perts[f] + change[:members]
                    means[f] = means[f] + change[members : members + 1]
            for f in range(fields):
                x = means[f] + perts[f]
                for d in range(2):
                    lines[pl.ds(f * members * high + 2 * p + d, members, stride=high), :] = x[:, d * tcols : (d + 1) * tcols]
            return carry

        lax.fori_loop(0, high // 2, pair, 0)

    most = jnp.maximum(active_ref[0], active_ref[1])

    @pl.when(most <= third)
    def _():
        run(third)

    @pl.when((most > third) & (most <= tcols))
    def _():
        run(tcols)

    @pl.when(most > tcols)
    def _():
        run(depth)


def on_device(n_lat, n_lon, ensemble, courant_cols, courant_rows, obs_value, obs_error, obs_cell, obs_kind, obs_live, obs_list):
    fields, members, trows, tcols = ensemble.shape
    slots = obs_value.shape[1]
    f32, i32 = jnp.float32, jnp.int32
    vmem = pl.BlockSpec(memory_space=pltpu.VMEM)
    smem = pl.BlockSpec(memory_space=pltpu.SMEM)
    lines = ensemble.reshape(fields * members * trows, tcols)
    raw = (lines, courant_cols, courant_rows, obs_value, obs_error, obs_live, obs_cell, obs_list)
    state, sides, tables = pl.pallas_call(
        functools.partial(exchange_kernel, (fields, members, trows, tcols, slots, n_lat, n_lon)),
        out_shape=(
            jax.ShapeDtypeStruct((fields * trows, members, tcols), f32),
            jax.ShapeDtypeStruct((2, members, tcols), f32),
            jax.ShapeDtypeStruct((2, 9, slots, tcols), f32),
        ),
        in_specs=[pl.BlockSpec(memory_space=pl.ANY)] * len(raw) + [smem, smem],
        out_specs=(vmem, vmem, vmem),
        scratch_shapes=[pltpu.VMEM(part.shape, part.dtype) for part in raw] + [
            pltpu.VMEM((2, EXTRA, tcols), f32),
            pltpu.VMEM((2, slots, tcols), f32),
            pltpu.VMEM((fields, trows + 2, members, tcols), f32),
            pltpu.VMEM((2, members, tcols), f32),
            pltpu.VMEM((2, members, tcols), f32),
            pltpu.VMEM((2, 9, slots, tcols), f32),
            pltpu.SemaphoreType.DMA((len(raw),)),
        ] + [pltpu.SemaphoreType.DMA((2,))] * 4 + [pltpu.SemaphoreType.DMA((2, 9))] * 2,
        compiler_params=pltpu.CompilerParams(
            collective_id=0, has_side_effects=True, vmem_limit_bytes=40 * 2**20),
        name="exchange",
    )(*raw, obs_cell, obs_kind)

    high = 8
    depth = -(-9 * slots // 16) * 16
    tall = -(-(members + 1) // 16) * 16
    wide = -(-3 * members // tcols) * tcols
    return pl.pallas_call(
        functools.partial(update_kernel, (fields, members, trows, tcols, slots, high)),
        grid=(trows // high,),
        out_shape=jax.ShapeDtypeStruct(ensemble.shape, f32),
        in_specs=[
            pl.BlockSpec((fields, high, members, tcols), lambda i: (0, i, 0, 0)),
            pl.BlockSpec((2, members, tcols), lambda i: (0, 0, 0)),
            pl.BlockSpec((2, 9, slots, tcols), lambda i: (0, 0, 0, 0)),
        ],
        out_specs=pl.BlockSpec((fields, members, high, tcols), lambda i: (0, 0, i, 0)),
        scratch_shapes=[
            pltpu.VMEM((2, depth, wide), jnp.bfloat16),
            pltpu.VMEM((2, 2 * tall, depth), jnp.bfloat16),
            pltpu.VMEM((2, tall, 2 * tcols), jnp.bfloat16),
            pltpu.VMEM((2, 2 * tall, 2 * tcols), jnp.bfloat16),
            pltpu.VMEM((2, depth, tcols), f32),
            pltpu.VMEM((2, depth, tcols), f32),
            pltpu.SMEM((2,), i32),
        ],
        compiler_params=pltpu.CompilerParams(vmem_limit_bytes=40 * 2**20),
        name="update",
    )(state.reshape(fields, trows, members, tcols), sides, tables)


def solution(mesh):
    placed = (
        P(None, None, "lat", "lon"),
        P(None, "lat", "lon"),
        P(None, "lat", "lon"),
        P(None, ("lat", "lon")),
        P(None, ("lat", "lon")),
        P(None, ("lat", "lon")),
        P(None, ("lat", "lon")),
        P(None, ("lat", "lon")),
        P(None, ("lat", "lon"), None),
    )
    return jax.shard_map(
        functools.partial(on_device, mesh.shape["lat"], mesh.shape["lon"]),
        mesh=mesh,
        in_specs=placed,
        out_specs=P(None, None, "lat", "lon"),
        check_vma=False,
    )
```

time: 69.2 us -> 47.9 us (0.69)
  Pallas kernels: 62.2 us -> 39.7 us
  local copies, waits for them, and re-layouts: 4.38 us -> 7.72 us
  other arithmetic: 2.1 us -> 0 us
    pallas_call x1, Pallas kernels: 32.5 us -> 18.4 us  [on_device(): pl.pallas_call(functools.partial(update_kernel, (fields, members, trows,...]
    pallas_call x1, Pallas kernels: 29.7 us -> 21.3 us  [on_device(): pl.pallas_call(functools.partial(exchange_kernel, (fields, members, trows...]
    unnamed x6 -> x17, local copies, waits for them, and re-layouts: 3.54 us -> 7.72 us
    convert_element_type x4 -> x0, other arithmetic: 2.09 us -> none  [the longest x1 0.71 us: on_device(): col.astype(f32)]
    concatenate x1 -> x0, local copies, waits for them, and re-layouts: 0.83 us -> none  [on_device(): jnp.concatenate([jnp.stack([obs_value, obs_live.astype(f32), obs_error, r...]
where the time goes in v1:
time: 47.9 us; the launch traced here: 47.4 us
  Pallas kernels  39.7 us (83%)
  local copies, waits for them, and re-layouts  7.72 us (16%)
    pallas_call x1, Pallas kernels, on_device(): pl.pallas_call(functools.partial(exchange_kernel, (fields, members, trows...  21.3 us
    pallas_call x1, Pallas kernels, on_device(): pl.pallas_call(functools.partial(update_kernel, (fields, members, trows,...  18.4 us
    unnamed x17, local copies, waits for them, and re-layouts  7.72 us

profile of v1, /device:TPU:1, one launch (start us, length us, event | category | flops | bytes accessed | tf_op | source)
XLA Modules:
  0.0 47.4 jit_solution(7901915294519774470)
XLA Ops:
  0.0 0.8 %copy.10.list_hbm = s32[2,24,9]{2,1,0:T(8,128)S(1)} copy(s32[2,24,9]{1,0,2:T(2,128)} %param.17) | data formatting | bytes 3456 | tf_op args[8]
  0.8 0.0 copy-start
  0.8 2.1 %copy-done = f32[3,80,32,128]{3,2,1,0:T(8,128)S(1)} copy-done((f32[3,80,32,128]{3,2,1,0:T(8,128)S(1)}, f32[3,80,32,128]{3,2,1,0:T(8,128)}, u32[]{:S(2)}) %copy-start) | copy-done | bytes 3932184
  2.9 0.0 copy-start.1
  2.9 0.7 %copy-done.1 = f32[1,32,128]{2,1,0:T(8,128)S(1)} copy-done((f32[1,32,128]{2,1,0:T(8,128)S(1)}, f32[1,32,128]{2,1,0:T(8,128)}, u32[]{:S(2)}) %copy-start.1) | copy-done | bytes 16408
  3.6 0.0 copy-start.2
  3.6 0.7 %copy-done.2 = f32[1,32,128]{2,1,0:T(8,128)S(1)} copy-done((f32[1,32,128]{2,1,0:T(8,128)S(1)}, f32[1,32,128]{2,1,0:T(8,128)}, u32[]{:S(2)}) %copy-start.2) | copy-done | bytes 16408
  4.3 0.0 copy-start.3
  4.3 0.7 %copy-done.3 = s32[2,24]{1,0:T(2,128)S(1)} copy-done((s32[2,24]{1,0:T(2,128)S(1)}, s32[2,24]{1,0:T(2,128)}, u32[]{:S(2)}) %copy-start.3) | copy-done | bytes 216
  5.0 0.0 copy-start.4
  5.0 0.7 %copy-done.4 = f32[2,24]{1,0:T(2,128)S(1)} copy-done((f32[2,24]{1,0:T(2,128)S(1)}, f32[2,24]{1,0:T(2,128)}, u32[]{:S(2)}) %copy-start.4) | copy-done | bytes 216
  5.7 0.0 copy-start.5
  5.7 0.7 %copy-done.5 = f32[2,24]{1,0:T(2,128)S(1)} copy-done((f32[2,24]{1,0:T(2,128)S(1)}, f32[2,24]{1,0:T(2,128)}, u32[]{:S(2)}) %copy-start.5) | copy-done | bytes 216
  6.4 0.0 copy-start.6
  6.4 0.7 %copy-done.6 = s32[2,24]{1,0:T(2,128)S(1)} copy-done((s32[2,24]{1,0:T(2,128)S(1)}, s32[2,24]{1,0:T(2,128)}, u32[]{:S(2)}) %copy-start.6) | copy-done | bytes 216
  7.0 0.0 copy-start.7
  7.1 0.7 %copy-done.7 = s32[2,24]{1,0:T(2,128)S(1)} copy-done((s32[2,24]{1,0:T(2,128)S(1)}, s32[2,24]{1,0:T(2,128)}, u32[]{:S(2)}) %copy-start.7) | copy-done | bytes 216
  7.7 21.3 %exchange.1 = (f32[96,80,128]{2,1,0:T(8,128)S(1)}, f32[2,80,128]{2,1,0:T(8,128)S(1)}, f32[2,9,24,128]{3,2,1,0:T(8,128)S(1)}) custom-call(f32[7680,128]{1,0:T(8,128)S(1)} %bitcast.3, f32[1,32,128]{2,1,0:T(8,128)S(1)} %copy-done.1, f32[1,32,128]{2,1,0:T(8,128)S(1)} %copy-done.2, f32[2,24]{1,0:T(2,128)S(1)} %copy-done.4, f32[2,24]{1,0:T(2,128)S(1)} %copy-done.5, ...), custom_call_target="tpu_custom_call" | custom-call | tf_op jit(solution)/shard_map/exchange/pallas_call | solution.py:434
  29.0 18.4 %update.1 = f32[3,80,32,128]{3,2,1,0:T(8,128)} custom-call(f32[3,32,80,128]{3,2,1,0:T(8,128)S(1)} %bitcast.2, f32[2,80,128]{2,1,0:T(8,128)S(1)} %get-tuple-element.9.sides_ref, f32[2,9,24,128]{3,2,1,0:T(8,128)S(1)} %get-tuple-element.10.tables_ref), custom_call_target="tpu_custom_call" | custom-call | tf_op jit(solution)/shard_map/update/pallas_call | solution.py:461
Async XLA Ops:
  0.8 2.1 %copy-start = (f32[3,80,32,128]{3,2,1,0:T(8,128)S(1)}, f32[3,80,32,128]{3,2,1,0:T(8,128)}, u32[]{:S(2)}) copy-start(f32[3,80,32,128]{3,2,1,0:T(8,128)} %param.9) | copy-start | bytes 11796484
  2.9 0.7 %copy-start.1 = (f32[1,32,128]{2,1,0:T(8,128)S(1)}, f32[1,32,128]{2,1,0:T(8,128)}, u32[]{:S(2)}) copy-start(f32[1,32,128]{2,1,0:T(8,128)} %cu_hbm.1) | copy-start | bytes 49156
  3.6 0.7 %copy-start.2 = (f32[1,32,128]{2,1,0:T(8,128)S(1)}, f32[1,32,128]{2,1,0:T(8,128)}, u32[]{:S(2)}) copy-start(f32[1,32,128]{2,1,0:T(8,128)} %cv_hbm.1) | copy-start | bytes 49156
  4.3 0.7 %copy-start.3 = (s32[2,24]{1,0:T(2,128)S(1)}, s32[2,24]{1,0:T(2,128)}, u32[]{:S(2)}) copy-start(s32[2,24]{1,0:T(2,128)} %cell_ref.1) | copy-start | bytes 580
  5.0 0.7 %copy-start.4 = (f32[2,24]{1,0:T(2,128)S(1)}, f32[2,24]{1,0:T(2,128)}, u32[]{:S(2)}) copy-start(f32[2,24]{1,0:T(2,128)} %value_hbm.1) | copy-start | bytes 580
  5.7 0.7 %copy-start.5 = (f32[2,24]{1,0:T(2,128)S(1)}, f32[2,24]{1,0:T(2,128)}, u32[]{:S(2)}) copy-start(f32[2,24]{1,0:T(2,128)} %error_hbm.1) | copy-start | bytes 580
  6.4 0.7 %copy-start.6 = (s32[2,24]{1,0:T(2,128)S(1)}, s32[2,24]{1,0:T(2,128)}, u32[]{:S(2)}) copy-start(s32[2,24]{1,0:T(2,128)} %live_hbm.1) | copy-start | bytes 580
  7.0 0.7 %copy-start.7 = (s32[2,24]{1,0:T(2,128)S(1)}, s32[2,24]{1,0:T(2,128)}, u32[]{:S(2)}) copy-start(s32[2,24]{1,0:T(2,128)} %kind_ref.1) | copy-start | bytes 580

commit v2 on v1

--- a/solution.py
+++ b/solution.py
@@ -55,9 +55,9 @@
 
 def exchange_kernel(
     sizes, x_hbm, cu_hbm, cv_hbm, value_hbm, error_hbm, live_hbm, cell_hbm, list_hbm, cell_ref, kind_ref,
-    state_ref, sides_ref, tables_ref,
-    x_ref, cu_ref, cv_ref, value_ref, error_ref, live_ref, cells_ref, list_ref, info, listed,
-    xt, pack, halo, near, in_sem, row_send, row_recv, col_send, col_recv, tab_send, tab_recv,
+    state_hbm, sides_ref, tables_ref,
+    state_ref, x_ref, cu_ref, cv_ref, value_ref, error_ref, live_ref, cells_ref, list_ref, info,
+    xt, pack, halo, near, in_sem, row_send, row_recv, col_send, col_recv, tab_send, tab_recv, out_sem,
 ):
     fields, members, trows, tcols, slots, n_lat, n_lon = sizes
     lat, lon = lax.axis_index("lat"), lax.axis_index("lon")
@@ -66,10 +66,12 @@
         r, c = lat + a, lon + b
         return (r >= 0) & (r < n_lat) & (c >= 0) & (c < n_lon)
 
+    part = members * trows
+    own_field = [pl.ds(f * part, part) for f in range(fields)]
     loads = [
         pltpu.make_async_copy(src, dst, in_sem.at[k])
-        for k, (src, dst) in enumerate([
-            (x_hbm, x_ref), (cu_hbm, cu_ref), (cv_hbm, cv_ref), (value_hbm, value_ref), (error_hbm, error_ref),
+        for k, (src, dst) in enumerate([(x_hbm.at[own], x_ref.at[own]) for own in own_field] + [
+            (cu_hbm, cu_ref), (cv_hbm, cv_ref), (value_hbm, value_ref), (error_hbm, error_ref),
             (live_hbm, live_ref), (cell_hbm, cells_ref), (list_hbm, list_ref)])
     ]
     for copy in loads:
@@ -80,7 +82,6 @@
     halo[...] = jnp.zeros(halo.shape, jnp.float32)
     near[...] = jnp.zeros(near.shape, jnp.float32)
     info[...] = jnp.ones(info.shape, jnp.float32)
-    listed[...] = jnp.zeros(listed.shape, jnp.float32)
 
     barrier = pltpu.get_barrier_semaphore()
     for a, b in AROUND:
@@ -89,21 +90,21 @@
             pl.semaphore_signal(barrier, inc=1, device_id=(lat + a, lon + b), device_id_type=MESH)
 
     lane = lax.broadcasted_iota(jnp.int32, (members, tcols), 1)
-    for copy in loads:
-        copy.wait()
-
-    def turn(i, carry):
+
+    def turn(f, i, carry):
         west, east = carry
-        for f in range(fields):
-            tile = x_ref[pl.ds(f * members * trows + i, members, stride=trows), :]
-            xt[f, i + 1] = tile
-            here = lane == f * trows + i
-            west = jnp.where(here, jnp.broadcast_to(tile[:, 0:1], tile.shape), west)
-            east = jnp.where(here, jnp.broadcast_to(tile[:, tcols - 1 : tcols], tile.shape), east)
+        tile = x_ref[pl.ds(f * part + i, members, stride=trows), :]
+        xt[f, i + 1] = tile
+        here = lane == f * trows + i
+        west = jnp.where(here, jnp.broadcast_to(tile[:, 0:1], tile.shape), west)
+        east = jnp.where(here, jnp.broadcast_to(tile[:, tcols - 1 : tcols], tile.shape), east)
         return west, east
 
     none = jnp.zeros((members, tcols), jnp.float32)
-    west, east = lax.fori_loop(0, trows, turn, (none, none), unroll=2)
+    west, east = none, none
+    for f in range(fields):
+        loads[f].wait()
+        west, east = lax.fori_loop(0, trows, functools.partial(turn, f), (west, east), unroll=4)
     pack[0] = west
     pack[1] = east
 
@@ -134,6 +135,9 @@
         @pl.when(exists(d, 0))
         def _():
             row_copy(k).start()
+
+    for copy in loads[fields:]:
+        copy.wait()
 
     def advect(i, carry):
         u = jnp.broadcast_to(cu_ref[0, pl.ds(i, 1), :], (members, tcols))
@@ -152,7 +156,7 @@
             state_ref[f * trows + i] = out
         return carry
 
-    lax.fori_loop(1, trows - 1, advect, 0)
+    lax.fori_loop(1, trows - 1, advect, 0, unroll=2)
 
     for batch in range(2):
         own = pl.ds(0, slots)
@@ -163,7 +167,8 @@
         row = jnp.floor((cells.astype(jnp.float32) + 0.5) * (1.0 / tcols))
         info[batch, 3:4, own] = row
         info[batch, 4:5, own] = cells.astype(jnp.float32) - row * tcols
-        listed[batch, :, 0 : list_ref.shape[2]] = list_ref[batch].astype(jnp.float32)
+        for k in range(list_ref.shape[0]):
+            info[batch, 5 + k : 6 + k, own] = list_ref[k, batch : batch + 1, :].astype(jnp.float32)
 
     def along(column):
         spread = jnp.broadcast_to(column, (trows, tcols))
@@ -196,6 +201,8 @@
 
     advect(0, 0)
     advect(trows - 1, 0)
+    keep = pltpu.make_async_copy(state_ref, state_hbm, out_sem)
+    keep.start()
     first_add = halo[1] * rise
     last_add = halo[0] * fall
     sides_ref[0] = first_add
@@ -226,10 +233,7 @@
         )
 
     def send(batch, prior):
-        table = make_table(prior, info[batch])[:slots]
-        at = lax.broadcasted_iota(jnp.int32, table.shape, 1)
-        table = jnp.where(at < members + 5, table, pltpu.roll(listed[batch], members + 5, 1))
-        near[batch, slot_of(0, 0)] = table
+        near[batch, slot_of(0, 0)] = make_table(prior, info[batch])[:slots]
         for a, b in AROUND:
             @pl.when(exists(a, b))
             def _():
@@ -270,6 +274,7 @@
     send(1, mean + pert - change)
     finish(1)
     tables_ref[...] = near[...]
+    keep.wait()
 
 
 def split(x):
@@ -358,35 +363,36 @@
         def zero_rows(rows):
             return [jnp.zeros((rows, 2 * tcols), jnp.bfloat16)] if rows else []
 
-        def pair(p, carry):
-            row = step * high + 2 * p
-            loc = []
-            for batch in range(2):
-                parts = []
-                for d in range(2):
-                    z = (rowrel[batch, 0:taken] - (row + d).astype(jnp.float32)) * (1.0 / trows)
-                    parts.append(taper(z) * colw[batch, 0:taken])
-                loc.append(jnp.concatenate(parts, axis=1))
-            xs = []
-            for f in range(fields):
-                tiles = []
-                for d in range(2):
-                    at = f * trows + row + d
-                    first = pltpu.roll(sides_ref[0], lax.rem(tcols - at, tcols), 1)
-                    last = pltpu.roll(sides_ref[1], tcols - 1 - at, 1)
-                    add = jnp.where(lane == 0, first, jnp.where(lane == tcols - 1, last, 0.0))
-                    tiles.append(state_ref[f, 2 * p + d] + add)
-                xs.append(jnp.concatenate(tiles, axis=1))
+        def pairs(q, carry):
+            locs, xs = [], []
+            for p in range(together):
+                row = step * high + 2 * (together * q + p)
+                locs.append([])
+                for batch in range(2):
+                    parts = []
+                    for d in range(2):
+                        z = (rowrel[batch, 0:taken] - (row + d).astype(jnp.float32)) * (1.0 / trows)
+                        parts.append(taper(z) * colw[batch, 0:taken])
+                    locs[p].append(jnp.concatenate(parts, axis=1))
+                for f in range(fields):
+                    tiles = []
+                    for d in range(2):
+                        at = f * trows + row + d
+                        first = pltpu.roll(sides_ref[0], lax.rem(tcols - at, tcols), 1)
+                        last = pltpu.roll(sides_ref[1], tcols - 1 - at, 1)
+                        add = jnp.where(lane == 0, first, jnp.where(lane == tcols - 1, last, 0.0))
+                        tiles.append(state_ref[f, 2 * (together * q + p) + d] + add)
+                    xs.append(jnp.concatenate(tiles, axis=1))
             means = [jnp.sum(x, axis=0, keepdims=True) * (1.0 / members) for x in xs]
             perts = [x - mean for x, mean in zip(xs, means)]
             for batch in range(2):
                 projs = []
-                for f in range(fields):
-                    hi, lo = split(perts[f])
+                for k in range(len(xs)):
+                    hi, lo = split(perts[k])
                     right = jnp.concatenate([hi, hi, lo] + zero_rows(wide - 3 * members), axis=0)
                     projs.append(jnp.dot(left[batch, 0:taken], right, preferred_element_type=jnp.float32))
-                for f in range(fields):
-                    w_hi, w_lo = split(projs[f] * loc[batch])
+                for k in range(len(xs)):
+                    w_hi, w_lo = split(projs[k] * locs[k // fields][batch])
                     if taken == third:
                         stack = jnp.concatenate([w_hi, w_hi, w_lo] + zero_rows(2 * tcols - 3 * third), axis=0)
                         change = jnp.dot(back3[batch], stack, preferred_element_type=jnp.float32)
@@ -398,15 +404,17 @@
                         one = jnp.dot(back[batch], w_hi, preferred_element_type=jnp.float32)
                         two = jnp.dot(back[batch, 0:tall], w_lo, preferred_element_type=jnp.float32)
                         change = one[:tall] + one[tall:] + two
-                    perts[f] = perts[f] + change[:members]
-                    means[f] = means[f] + change[members : members + 1]
-            for f in range(fields):
-                x = means[f] + perts[f]
+                    perts[k] = perts[k] + change[:members]
+                    means[k] = means[k] + change[members : members + 1]
+            for k in range(len(xs)):
+                x = means[k] + perts[k]
                 for d in range(2):
-                    lines[pl.ds(f * members * high + 2 * p + d, members, stride=high), :] = x[:, d * tcols : (d + 1) * tcols]
+                    start = (k % fields) * members * high + 2 * (together * q + k // fields) + d
+                    lines[pl.ds(start, members, stride=high), :] = x[:, d * tcols : (d + 1) * tcols]
             return carry
 
-        lax.fori_loop(0, high // 2, pair, 0)
+        together = 2 if taken == third else 1
+        lax.fori_loop(0, high // (2 * together), pairs, 0)
 
     most = jnp.maximum(active_ref[0], active_ref[1])
 
@@ -430,7 +438,7 @@
     vmem = pl.BlockSpec(memory_space=pltpu.VMEM)
     smem = pl.BlockSpec(memory_space=pltpu.SMEM)
     lines = ensemble.reshape(fields * members * trows, tcols)
-    raw = (lines, courant_cols, courant_rows, obs_value, obs_error, obs_live, obs_cell, obs_list)
+    raw = (lines, courant_cols, courant_rows, obs_value, obs_error, obs_live, obs_cell, jnp.transpose(obs_list, (2, 0, 1)))
     state, sides, tables = pl.pallas_call(
         functools.partial(exchange_kernel, (fields, members, trows, tcols, slots, n_lat, n_lon)),
         out_shape=(
@@ -438,19 +446,18 @@
             jax.ShapeDtypeStruct((2, members, tcols), f32),
             jax.ShapeDtypeStruct((2, 9, slots, tcols), f32),
         ),
-        in_specs=[pl.BlockSpec(memory_space=pl.ANY)] * len(raw) + [smem, smem],
-        out_specs=(vmem, vmem, vmem),
-        scratch_shapes=[pltpu.VMEM(part.shape, part.dtype) for part in raw] + [
+        in_specs=[pl.BlockSpec(memory_space=pltpu.HBM)] * len(raw) + [smem, smem],
+        out_specs=(pl.BlockSpec(memory_space=pltpu.HBM), vmem, vmem),
+        scratch_shapes=[pltpu.VMEM((fields * trows, members, tcols), f32)] + [pltpu.VMEM(part.shape, part.dtype) for part in raw] + [
             pltpu.VMEM((2, EXTRA, tcols), f32),
-            pltpu.VMEM((2, slots, tcols), f32),
             pltpu.VMEM((fields, trows + 2, members, tcols), f32),
             pltpu.VMEM((2, members, tcols), f32),
             pltpu.VMEM((2, members, tcols), f32),
             pltpu.VMEM((2, 9, slots, tcols), f32),
-            pltpu.SemaphoreType.DMA((len(raw),)),
-        ] + [pltpu.SemaphoreType.DMA((2,))] * 4 + [pltpu.SemaphoreType.DMA((2, 9))] * 2,
+            pltpu.SemaphoreType.DMA((len(raw) - 1 + fields,)),
+        ] + [pltpu.SemaphoreType.DMA((2,))] * 4 + [pltpu.SemaphoreType.DMA((2, 9))] * 2 + [pltpu.SemaphoreType.DMA],
         compiler_params=pltpu.CompilerParams(
-            collective_id=0, has_side_effects=True, vmem_limit_bytes=40 * 2**20),
+            collective_id=0, has_side_effects=True, vmem_limit_bytes=64 * 2**20),
         name="exchange",
     )(*raw, obs_cell, obs_kind)
 
@@ -477,7 +484,7 @@
             pltpu.VMEM((2, depth, tcols), f32),
             pltpu.SMEM((2,), i32),
         ],
-        compiler_params=pltpu.CompilerParams(vmem_limit_bytes=40 * 2**20),
+        compiler_params=pltpu.CompilerParams(vmem_limit_bytes=64 * 2**20),
         name="update",
     )(state.reshape(fields, trows, members, tcols), sides, tables)
 

time: 47.9 us -> 35.9 us (0.75)
  local copies, waits for them, and re-layouts: 7.72 us -> 0 us
  Pallas kernels: 39.7 us -> 35.7 us
    unnamed x17 -> x0, local copies, waits for them, and re-layouts: 7.72 us -> none
    pallas_call x1, Pallas kernels: 18.4 us -> 13.6 us  [on_device(): pl.pallas_call(functools.partial(update_kernel, (fields, members, trows,...]
    pallas_call x1, Pallas kernels: 21.3 us -> 22.1 us  [on_device(): pl.pallas_call(functools.partial(exchange_kernel, (fields, members, trows...]
where the time goes in v2:
time: 35.9 us; the launch traced here: 35.7 us
  Pallas kernels  35.7 us (99%)
    pallas_call x1, Pallas kernels, on_device(): pl.pallas_call(functools.partial(exchange_kernel, (fields, members, trows...  22.1 us
    pallas_call x1, Pallas kernels, on_device(): pl.pallas_call(functools.partial(update_kernel, (fields, members, trows,...  13.6 us

profile of v2, /device:TPU:1, one launch (start us, length us, event | category | flops | bytes accessed | tf_op | source)
XLA Modules:
  0.0 35.7 jit_solution(7273209308629262052)
XLA Ops:
  0.0 22.1 %exchange.1 = (f32[96,80,128]{2,1,0:T(8,128)}, f32[2,80,128]{2,1,0:T(8,128)}, f32[2,9,24,128]{3,2,1,0:T(8,128)}) custom-call(f32[7680,128]{1,0:T(8,128)} %bitcast.4, f32[1,32,128]{2,1,0:T(8,128)} %cu_hbm.1, f32[1,32,128]{2,1,0:T(8,128)} %cv_hbm.1, f32[2,24]{1,0:T(2,128)} %value_hbm.1, f32[2,24]{1,0:T(2,128)} %error_hbm.1, s32[2,24]{1,0:T(2,128)} %live_hbm.1, ...), custom_call_target="tpu_custom_call" | custom-call | tf_op jit(solution)/shard_map/exchange/pallas_call | solution.py:442
  22.1 13.6 %update.1 = f32[3,80,32,128]{3,2,1,0:T(8,128)} custom-call(f32[3,32,80,128]{3,2,1,0:T(8,128)} %bitcast.3, f32[2,80,128]{2,1,0:T(8,128)} %get-tuple-element.9.sides_ref, f32[2,9,24,128]{3,2,1,0:T(8,128)} %get-tuple-element.10.tables_ref), custom_call_target="tpu_custom_call" | custom-call | tf_op jit(solution)/shard_map/update/pallas_call | solution.py:468

commit v3 on v2

--- a/solution.py
+++ b/solution.py
@@ -139,21 +139,22 @@
     for copy in loads[fields:]:
         copy.wait()
 
+    edge = lax.broadcasted_iota(jnp.int32, (8, tcols), 1)
+
     def advect(i, carry):
-        u = jnp.broadcast_to(cu_ref[0, pl.ds(i, 1), :], (members, tcols))
-        v = jnp.broadcast_to(cv_ref[0, pl.ds(i, 1), :], (members, tcols))
+        u = jnp.broadcast_to(cu_ref[0, pl.ds(i, 1), :], (8, tcols))
+        v = jnp.broadcast_to(cv_ref[0, pl.ds(i, 1), :], (8, tcols))
         hu, hv = 0.5 * u, 0.5 * v
         huu, hvv = hu * u, hv * v
+        all_of = lambda c: jnp.concatenate([c] * (members // 8), axis=0)
+        c_mid = all_of(1.0 - 2.0 * (huu + hvv))
+        c_east = all_of(jnp.where(edge == tcols - 1, 0.0, huu - hu))
+        c_west = all_of(jnp.where(edge == 0, 0.0, huu + hu))
+        c_north, c_south = all_of(hvv - hv), all_of(hvv + hv)
         for f in range(fields):
             mid = xt[f, i + 1]
-            south = xt[f, i]
-            north = xt[f, i + 2]
-            east = jnp.where(lane == tcols - 1, 0.0, pltpu.roll(mid, tcols - 1, 1))
-            west = jnp.where(lane == 0, 0.0, pltpu.roll(mid, 1, 1))
-            two = 2.0 * mid
-            out = mid - hu * (east - west) + huu * (east - two + west)
-            out = out - hv * (north - south) + hvv * (north - two + south)
-            state_ref[f * trows + i] = out
+            across = c_east * pltpu.roll(mid, tcols - 1, 1) + c_west * pltpu.roll(mid, 1, 1)
+            state_ref[f * trows + i] = c_mid * mid + across + (c_north * xt[f, i + 2] + c_south * xt[f, i])
         return carry
 
     lax.fori_loop(1, trows - 1, advect, 0, unroll=2)
@@ -413,7 +414,7 @@
                     lines[pl.ds(start, members, stride=high), :] = x[:, d * tcols : (d + 1) * tcols]
             return carry
 
-        together = 2 if taken == third else 1
+        together = high // 2 if taken == third else 1
         lax.fori_loop(0, high // (2 * together), pairs, 0)
 
     most = jnp.maximum(active_ref[0], active_ref[1])

time: 35.9 us -> 34 us (0.947)
  Pallas kernels: 35.7 us -> 33.8 us
    pallas_call x1, Pallas kernels: 13.6 us -> 11.7 us  [on_device(): pl.pallas_call(functools.partial(update_kernel, (fields, members, trows,...]
where the time goes in v3:
time: 34 us; the launch traced here: 33.8 us
  Pallas kernels  33.8 us (99%)
    pallas_call x1, Pallas kernels, on_device(): pl.pallas_call(functools.partial(exchange_kernel, (fields, members, trows...  22.1 us
    pallas_call x1, Pallas kernels, on_device(): pl.pallas_call(functools.partial(update_kernel, (fields, members, trows,...  11.7 us

profile of v3, /device:TPU:1, one launch (start us, length us, event | category | flops | bytes accessed | tf_op | source)
XLA Modules:
  0.0 33.8 jit_solution(8916333962373592739)
XLA Ops:
  0.0 22.1 %exchange.1 = (f32[96,80,128]{2,1,0:T(8,128)}, f32[2,80,128]{2,1,0:T(8,128)}, f32[2,9,24,128]{3,2,1,0:T(8,128)}) custom-call(f32[7680,128]{1,0:T(8,128)} %bitcast.4, f32[1,32,128]{2,1,0:T(8,128)} %cu_hbm.1, f32[1,32,128]{2,1,0:T(8,128)} %cv_hbm.1, f32[2,24]{1,0:T(2,128)} %value_hbm.1, f32[2,24]{1,0:T(2,128)} %error_hbm.1, s32[2,24]{1,0:T(2,128)} %live_hbm.1, ...), custom_call_target="tpu_custom_call" | custom-call | tf_op jit(solution)/shard_map/exchange/pallas_call | solution.py:443
  22.1 11.7 %update.1 = f32[3,80,32,128]{3,2,1,0:T(8,128)} custom-call(f32[3,32,80,128]{3,2,1,0:T(8,128)} %bitcast.3, f32[2,80,128]{2,1,0:T(8,128)} %get-tuple-element.9.sides_ref, f32[2,9,24,128]{3,2,1,0:T(8,128)} %get-tuple-element.10.tables_ref), custom_call_target="tpu_custom_call" | custom-call | tf_op jit(solution)/shard_map/update/pallas_call | solution.py:469

commit v4 on v3

--- a/solution.py
+++ b/solution.py
@@ -331,7 +331,12 @@
             running = jnp.dot(line, upper, preferred_element_type=jnp.float32)[0:1]
             active_ref[batch] = jnp.max(running).astype(jnp.int32)
             pick = jnp.where((running - 1.0 == r.astype(jnp.float32)) & (flags > 0.5), 1.0, 0.0)
-            whole = jnp.dot(pick, whole, precision=HIGHEST, preferred_element_type=jnp.float32)
+            pick = pick.astype(jnp.bfloat16)
+            top, rest = whole.astype(jnp.bfloat16), whole
+            rest = rest - top.astype(jnp.float32)
+            middle, last = split(rest)
+            picked = jnp.dot(pick, jnp.concatenate([top, middle], axis=1), preferred_element_type=jnp.float32)
+            whole = picked[:, :tcols] + picked[:, tcols:] + jnp.dot(pick, last, preferred_element_type=jnp.float32)
 
             lane = lax.broadcasted_iota(jnp.int32, whole.shape, 1)
             yp = jnp.where(lane < members, whole, 0.0)

time: 34 us -> 33.8 us (level)
  no operation moved by 1% of the time
where the time goes in v4:
time: 33.8 us; the launch traced here: 33.7 us
  Pallas kernels  33.7 us (100%)
    pallas_call x1, Pallas kernels, on_device(): pl.pallas_call(functools.partial(exchange_kernel, (fields, members, trows...  22.1 us
    pallas_call x1, Pallas kernels, on_device(): pl.pallas_call(functools.partial(update_kernel, (fields, members, trows,...  11.6 us

profile of v4, /device:TPU:1, one launch (start us, length us, event | category | flops | bytes accessed | tf_op | source)
XLA Modules:
  0.0 33.7 jit_solution(14064958499035160307)
XLA Ops:
  0.0 22.1 %exchange.1 = (f32[96,80,128]{2,1,0:T(8,128)}, f32[2,80,128]{2,1,0:T(8,128)}, f32[2,9,24,128]{3,2,1,0:T(8,128)}) custom-call(f32[7680,128]{1,0:T(8,128)} %bitcast.4, f32[1,32,128]{2,1,0:T(8,128)} %cu_hbm.1, f32[1,32,128]{2,1,0:T(8,128)} %cv_hbm.1, f32[2,24]{1,0:T(2,128)} %value_hbm.1, f32[2,24]{1,0:T(2,128)} %error_hbm.1, s32[2,24]{1,0:T(2,128)} %live_hbm.1, ...), custom_call_target="tpu_custom_call" | custom-call | tf_op jit(solution)/shard_map/exchange/pallas_call | solution.py:448
  22.1 11.6 %update.1 = f32[3,80,32,128]{3,2,1,0:T(8,128)} custom-call(f32[3,32,80,128]{3,2,1,0:T(8,128)} %bitcast.3, f32[2,80,128]{2,1,0:T(8,128)} %get-tuple-element.9.sides_ref, f32[2,9,24,128]{3,2,1,0:T(8,128)} %get-tuple-element.10.tables_ref), custom_call_target="tpu_custom_call" | custom-call | tf_op jit(solution)/shard_map/update/pallas_call | solution.py:474
